TPU v7x, 256 devices: a whole 4x4x8 slice. The times are simulated.
256 devices in a mesh: row: 8 (over y, core), band: 32 (over z, x).
Axes of the slice: x: 4, y: 4, z: 8, core: 2. Of those that a mesh axis runs over, the one named last changes fastest.
Arguments:
- coeffs: bfloat16 [8192, 16384], P('row', 'band'), may hold values from -0.046875 to 0.046875
- occupation: float32 [16384], P('band'), may hold values from 0.2 to 2
- tile_left: int32 [8, 8, 16], P('row'), may hold values from 0 to 7
- tile_right: int32 [8, 8, 16], P('row'), may hold values from 0 to 7
- owners: int32 [1024, 6], P(('row', 'band')), may hold values from 0 to 31, all different within a row; in each aligned block of 4 rows (0 to 3, 4 to 7, ...) at most 2 rows name the same one
- brick_slot: int32 [1024, 6], P(('row', 'band')), may hold values from 0 to 7
- patterns: int32 [1024, 6, 2], P(('row', 'band')), may hold values from 0 to 3
- basis_table: bfloat16 [4, 128, 2048], replicated, may hold values from -3 to 3
Outputs:
- density: float32 [2048, 2048], P(('row', 'band'))
Inputs may be any that keep to these rules, and one draw needn't show every extreme that they name: Each row names 6 different owners. Among the rows g from k * 4 to k * 4 + 4 - 1 (aligned blocks), no owner is named by more than 2 rows, a bound that some owner reaches in some of these blocks.
All inputs are finite; a program needn't handle non-finite values.
Results may differ from a plain program's by a relative error of at most 0.009.
Values may be sent and summed in bfloat16 or wider, within the bound.
A program may use at most 64 MiB of HBM per device.

v0:
```python
import jax
import jax.numpy as jnp
from jax import lax
from jax.sharding import PartitionSpec as P

BS = 128
NBR_DEV = 8


slot_group = 4


def collocate(blocks, left_rows, right_rows):
    products = jnp.einsum("sij,sjg->sig", blocks, right_rows, preferred_element_type=jnp.float32)
    return jnp.sum(left_rows.astype(jnp.float32) * products, axis=1)


def collocate_all(blocks, left_ids, right_ids, basis_table):
    count = blocks.shape[0]
    groups = count // slot_group
    width = blocks.shape[1]

    def one_group(items):
        group_blocks, group_left, group_right = items
        return collocate(group_blocks, basis_table[group_left], basis_table[group_right])

    result = lax.map(
        one_group,
        (
            blocks.reshape(groups, slot_group, width, width),
            left_ids.reshape(groups, slot_group),
            right_ids.reshape(groups, slot_group),
        ),
    )
    return result.reshape(count, basis_table.shape[2])


def body(coeffs, occupation, tile_left, tile_right, owners, brick_slot, patterns, basis_table):
    width = coeffs.shape[1]
    panel = coeffs.shape[0]
    blocks_here = panel // BS
    row_count = lax.axis_size("row")
    band_count = lax.axis_size("band")
    row_index = lax.axis_index("row")
    band_index = lax.axis_index("band")
    weighted = (coeffs.astype(jnp.float32) * occupation[None, :]).astype(jnp.bfloat16)
    weighted_blocks = weighted.reshape(blocks_here, BS, width)
    left_table = tile_left[0]
    right_table = tile_right[0]
    per_pair = left_table.shape[1]
    start_tiles = jnp.zeros((row_count, per_pair, BS, BS), jnp.float32)
    piece = lax.all_gather(coeffs, "row", axis=0, tiled=True)
    count = piece.shape[0] // panel
    pieces = piece.reshape(count, blocks_here, BS, width)

    def one_panel(index, current):
        rows_left = weighted_blocks[left_table[index]]
        rows_right = pieces[index][right_table[index]]
        block = jnp.einsum(
            "tik,tjk->tij", rows_left, rows_right, preferred_element_type=jnp.float32
        )
        return lax.dynamic_update_slice_in_dim(current, block[None], index, 0)

    tiles = lax.fori_loop(0, count, one_panel, start_tiles)
    flat = tiles.reshape(row_count * per_pair, BS, BS).astype(jnp.bfloat16)
    mine_count = owners.shape[0]
    summed = lax.psum_scatter(flat, "band", scatter_dimension=0, tiled=True).astype(jnp.float32)
    density_blocks = summed.astype(jnp.bfloat16)
    positions = band_index * mine_count + jnp.arange(mine_count, dtype=jnp.int32)
    column_panel = positions // per_pair
    same = (column_panel == row_index) & (
        left_table.reshape(-1)[positions] == right_table.reshape(-1)[positions]
    )
    weight_int = jnp.where(same, 1, 2).astype(jnp.int32)
    reach = owners.shape[1]
    entries = mine_count * reach
    owner_flat = owners.reshape(entries)
    slot_flat = brick_slot.reshape(entries)
    left_pattern = patterns[:, :, 0].reshape(entries)
    right_pattern = patterns[:, :, 1].reshape(entries)
    entry_tile = jnp.arange(entries, dtype=jnp.int32) // reach
    entry_weight = weight_int[entry_tile]
    capacity = min(mine_count, 2 * ((entries + band_count - 1) // band_count))
    owner_hits = (owner_flat[:, None] == jnp.arange(band_count, dtype=jnp.int32)[None, :]).astype(
        jnp.int32
    )
    rank = jnp.sum((jnp.cumsum(owner_hits, axis=0) - owner_hits) * owner_hits, axis=1)
    target = owner_flat * capacity + rank
    places = band_count * capacity
    select = jnp.arange(places, dtype=jnp.int32)[:, None] == target[None, :]
    entry_blocks = density_blocks[entry_tile].reshape(entries, BS * BS)
    outgoing = jnp.dot(
        select.astype(jnp.bfloat16), entry_blocks, preferred_element_type=jnp.float32
    ).astype(jnp.bfloat16)
    details = jnp.stack([slot_flat, left_pattern, right_pattern, entry_weight], axis=1)
    outgoing_details = jnp.zeros((places, 4), jnp.int32).at[target].set(details)
    blocks = lax.all_to_all(
        outgoing.reshape(band_count, capacity, BS * BS),
        "band",
        split_axis=0,
        concat_axis=0,
        tiled=True,
    )
    info = lax.all_to_all(
        outgoing_details.reshape(band_count, capacity, 4),
        "band",
        split_axis=0,
        concat_axis=0,
        tiled=True,
    )
    sources = info.shape[0]
    items = info.shape[1]
    flat_blocks = blocks.reshape(sources * items, BS, BS)
    flat_info = info.reshape(sources * items, 4)
    contrib = collocate_all(flat_blocks, flat_info[:, 1], flat_info[:, 2], basis_table)
    contrib = contrib * flat_info[:, 3].astype(jnp.float32)[:, None]
    arrived = contrib.reshape(sources, items, contrib.shape[1])
    brick_ids = flat_info[:, 0].reshape(sources, items)
    points = arrived.shape[-1]
    hits = (jnp.arange(NBR_DEV, dtype=jnp.int32)[:, None] == brick_ids.reshape(-1)[None, :]).astype(
        jnp.float32
    )
    return jnp.dot(hits, arrived.reshape(-1, points), precision=lax.Precision.HIGHEST)


def solution(mesh):
    return jax.shard_map(
        body,
        mesh=mesh,
        in_specs=(
            P("row", "band"),
            P("band"),
            P("row", None, None),
            P("row", None, None),
            P(("row", "band"), None),
            P(("row", "band"), None),
            P(("row", "band"), None, None),
            P(),
        ),
        out_specs=P(("row", "band"), None),
        check_vma=False,
    )
```

profile of v0, /device:TPU:32, one launch (start us, length us, event | category | flops | bytes accessed | tf_op | source)
XLA Modules:
  0.0 535.0 jit_solution(18292953927688108871)
XLA Ops:
  7.3 2.4 multiply_convert_fusion
  9.7 54.4 %all-gather.2.cloned.1.call-done = bf16[8192,512]{1,0:T(8,128)(2,1)} async-done(((bf16[1024,512]{1,0:T(8,128)(2,1)}), bf16[8192,512]{1,0:T(8,128)(2,1)}) %all-gather.2.cloned.1.call-update) | async-done | bytes 8388624 | tf_op jit(solution)/shard_map/all_gather | solution.py:52
  64.2 67.5 %while.23 = (s32[]{:T(128)}, bf16[8,16,128,128]{3,2,1,0:T(8,128)(2,1)}, s32[8,16]{1,0:T(8,128)S(1)}, bf16[8,128,512]{2,1,0:T(8,128)(2,1)}, bf16[8,8,128,512]{3,2...) while((s32[]{:T(128)}, bf16[8,16,128,128]{3,2,1,0:T(8,128)(2,1)}, s32[8,16]{1,0:T(8,128)S(1)}, ...), condition=%wide.region_4.5_spmd, body=%wide.region_3.4_spmd.sunk | while | flops 268437600 | bytes 15737941 | solution.py:64
  66.2 3.3 gather_fusion
  69.5 3.1 fusion.41
  74.7 3.3 gather_fusion
  78.0 3.2 fusion.41
  83.2 3.3 gather_fusion
  86.5 3.1 fusion.41
  91.6 3.3 gather_fusion
  94.9 3.1 fusion.41
  100.0 3.3 gather_fusion
  103.3 3.1 fusion.41
  108.5 3.3 gather_fusion
  111.7 3.1 fusion.41
  116.9 3.3 gather_fusion
  120.2 3.1 fusion.41
  125.3 3.3 gather_fusion
  128.6 3.1 fusion.41
  134.2 2.6 fusion.24
  138.5 10.1 %all-to-all-start = ((s32[32,2,4]{2,1,0:T(2,128)}), s32[32,2,4]{2,1,0:T(2,128)S(1)}, u32[]{:S(2)}, u32[]{:S(2)}) async-start(s32[32,2,4]{2,1,0:T(2,128)} %bitcast.21), calls=%async_computation | async-start | bytes 65536 | tf_op jit(solution)/shard_map/all_to_all | solution.py:104
  148.6 203.3 %reduce-scatter.2.cloned.1.call-done = bf16[4,128,128]{2,1,0:T(8,128)(2,1)} async-done(((bf16[128,128,128]{2,1,0:T(8,128)(2,1)}), bf16[4,128,128]{2,1,0:T(8,128)(2,1)}) %reduce-scatter.2.cloned.1.call-update) | async-done | bytes 131088 | tf_op jit(solution)/shard_map/reduce_scatter | solution.py:67
  354.3 2.7 reshape.243
  357.0 8.0 %all-to-all-start.1 = ((bf16[32,2,16384]{2,1,0:T(2,128)(2,1)}), bf16[32,2,16384]{2,1,0:T(2,128)(2,1)}, u32[]{:S(2)}, u32[]{:S(2)}) async-start(bf16[32,2,16384]{2,1,0:T(2,128)(2,1)} %reshape.243), calls=%async_computation.2 | async-start | bytes 4194304 | tf_op jit(solution)/shard_map/all_to_all | solution.py:97
  365.6 44.2 %all-to-all-done.1 = bf16[32,2,16384]{2,1,0:T(2,128)(2,1)} async-done(((bf16[32,2,16384]{2,1,0:T(2,128)(2,1)}), bf16[32,2,16384]{2,1,0:T(2,128)(2,1)}, u32[]{:S(2)}, u32[]{:S(2)}) %all-to-all-start.1) | async-done | bytes 2097184 | tf_op jit(solution)/shard_map/all_to_all | solution.py:97
  409.8 4.5 reshape_reshape.3
  414.3 112.7 %while.24 = (s32[]{:T(128)}, f32[16,4,2048]{2,1,0:T(4,128)S(1)}, s32[16,4]{1,0:T(8,128)S(1)}, bf16[4,128,2048]{2,1,0:T(8,128)(2,1)S(1)}, bf16[16,4,128,128]{3,2,...) while((s32[]{:T(128)}, f32[16,4,2048]{2,1,0:T(4,128)S(1)}, s32[16,4]{1,0:T(8,128)S(1)}, ...), condition=%wide.region_8.9_spmd, body=%wide.region_6.8_spmd.sunk | while | flops 271575072 | bytes 12821205 | solution.py:27
  416.3 2.0 gather_fusion.3
  418.3 3.0 multiply_reduce_fusion.2
  423.4 2.0 gather_fusion.3
  425.4 3.0 multiply_reduce_fusion.2
  430.4 2.0 gather_fusion.3
  432.4 3.0 multiply_reduce_fusion.2
  437.5 2.0 gather_fusion.3
  439.5 3.0 multiply_reduce_fusion.2
  446.5 3.0 multiply_reduce_fusion.2
  453.5 3.0 multiply_reduce_fusion.2
  460.6 3.0 multiply_reduce_fusion.2
  467.6 3.0 multiply_reduce_fusion.2
  474.7 3.0 multiply_reduce_fusion.2
  479.7 2.0 gather_fusion.3
  481.7 3.0 multiply_reduce_fusion.2
  488.8 3.0 multiply_reduce_fusion.2
  495.8 3.0 multiply_reduce_fusion.2
  502.8 3.0 multiply_reduce_fusion.2
  509.9 3.0 multiply_reduce_fusion.2
  516.9 3.0 multiply_reduce_fusion.2
  524.0 3.0 multiply_reduce_fusion.2
  (183 shorter events, 79.7 us)
Async XLA Ops:
  6.5 57.6 %copy-start.1 = (s32[1,8,16]{2,1,0:T(8,128)S(1)}, s32[1,8,16]{2,1,0:T(8,128)}, u32[]{:S(2)}) copy-start(s32[1,8,16]{2,1,0:T(8,128)} %param.14) | copy-start | bytes 1540
  6.5 57.6 %copy-start.2 = (s32[1,8,16]{2,1,0:T(8,128)S(1)}, s32[1,8,16]{2,1,0:T(8,128)}, u32[]{:S(2)}) copy-start(s32[1,8,16]{2,1,0:T(8,128)} %param.15) | copy-start | bytes 1540
  6.5 57.6 %all-gather.2.cloned.1.call-start = ((), (), s32[]{:S(2)}) async-start(), calls=%async_computation.3 | async-start | bytes 9437184 | tf_op jit(solution)/shard_map/all_gather | solution.py:52
  7.3 344.7 %reduce-scatter.2.cloned.1.call-start = ((), (), s32[]{:S(2)}) async-start(), calls=%async_computation.4 | async-start | bytes 4325376 | tf_op jit(solution)/shard_map/reduce_scatter | solution.py:67
  131.7 1.5 copy-start.4
  131.7 1.7 copy-start.5
  131.7 5.1 copy-start.3
  138.5 218.5 %all-to-all-start = ((s32[32,2,4]{2,1,0:T(2,128)}), s32[32,2,4]{2,1,0:T(2,128)S(1)}, u32[]{:S(2)}, u32[]{:S(2)}) async-start(s32[32,2,4]{2,1,0:T(2,128)} %bitcast.21), calls=%async_computation | async-start | bytes 65536 | tf_op jit(solution)/shard_map/all_to_all | solution.py:104
  357.0 52.8 %all-to-all-start.1 = ((bf16[32,2,16384]{2,1,0:T(2,128)(2,1)}), bf16[32,2,16384]{2,1,0:T(2,128)(2,1)}, u32[]{:S(2)}, u32[]{:S(2)}) async-start(bf16[32,2,16384]{2,1,0:T(2,128)(2,1)} %reshape.243), calls=%async_computation.2 | async-start | bytes 4194304 | tf_op jit(solution)/shard_map/all_to_all | solution.py:97
  365.6 48.8 %copy-start = (bf16[4,128,2048]{2,1,0:T(8,128)(2,1)S(1)}, bf16[4,128,2048]{2,1,0:T(8,128)(2,1)}, u32[]{:S(2)}) copy-start(bf16[4,128,2048]{2,1,0:T(8,128)(2,1)} %param.19) | copy-start | bytes 6291460
Sparse Core Ops, SparseCore 0:
  9.2 54.8 all-gather.1
  131.8 220.0 reduce-scatter.1
where the time goes:
time: 537 us; the launch traced here: 535 us
  waiting for transfers between devices  303 us (56%)
  local copies, waits for them, and re-layouts  119 us (22%)
  matrix products  74.3 us (14%)
  starting transfers between devices  18.1 us (3%)
  between operations  13.6 us (3%)
  other arithmetic  6.06 us (1%)
    reduce_scatter x1, waiting for transfers between devices, body(): lax.psum_scatter(flat, 'band', scatter_dimension=0, tiled=True)  203 us
    all_gather x1, waiting for transfers between devices, body(): piece = lax.all_gather(coeffs, 'row', axis=0, tiled=True)  54.4 us
    dot_general x16, matrix products, collocate(): jnp.einsum('sij,sjg->sig', blocks, right_rows, preferred_element_type=jnp...  47.6 us
    all_to_all x1, waiting for transfers between devices, body(): lax.all_to_all(outgoing.reshape(band_count, capacity, BS * BS), 'band', s...  44.2 us
    gather x16, local copies, waits for them, and re-layouts, one_group(): basis_table[group_right]  32.1 us
    gather x16, local copies, waits for them, and re-layouts, one_group(): basis_table[group_left]  31.6 us
    gather x8, local copies, waits for them, and re-layouts, one_panel(): rows_left = weighted_blocks[left_table[index]]  26.1 us
    dot_general x8, matrix products, one_panel(): jnp.einsum('tik,tjk->tij', rows_left, rows_right, preferred_element_type=...  24.9 us
  transfers between devices with their start and end apart: 4, of which 3 were waited for; matrix products, arithmetic and copies ran while one was open for 3% of the time, Pallas kernels for 0%

commit v1 on v0

v1 whole, which is shorter than its diff:
```python
import functools

import jax
import jax.numpy as jnp
from jax import lax
from jax.experimental import pallas as pl
from jax.experimental.pallas import tpu as pltpu
from jax.sharding import PartitionSpec as P

BS = 128
NBR = 8
TOP = 6
G = 2048
GS, GL = 16, 128
NTP = 16
BLOCKS = 8
KD = 512
NX, NY, NZ = 4, 4, 8
CHUNK = 512
Z_ORDER = (4, 3, 5, 2, 6, 1, 7)
X_ORDER = (2, 1, 3)
MESH = pl.DeviceIdType.MESH


def kernel(
    coeffs,
    occ,
    left,
    right,
    meta,
    basis,
    out,
    w,
    b0,
    f_a,
    f_b,
    s_a,
    s_b,
    t_a,
    t_b,
    tiles,
    x1_l,
    x1_r,
    x2_l,
    x2_r,
    zs,
    rz,
    terms,
    send_e,
    e1,
    arr,
    mx,
    mz,
    hits,
    meta_s,
    g_send,
    g_recv,
    x_send,
    x_recv,
    z_send,
    z_recv,
    e_send,
    e_recv,
    m_send,
    m_recv,
    l_sem,
):
    r = lax.axis_index("row")
    band = lax.axis_index("band")
    y, c = r // 2, r % 2
    z, x = band // NX, band % NX
    sg = 1 - 2 * c
    yp, ym, y2 = (y + sg + NY) % NY, (y - sg + NY) % NY, (y + 2) % NY
    oc = 1 - c
    xr, xl, x2 = (x + 1) % NX, (x + 3) % NX, (x + 2) % NX

    def dev_row(rr):
        return (rr, band)

    def dev_x(xx):
        return (r, z * NX + xx)

    def dev_z(zz):
        return (r, zz * NX + x)

    sib = dev_row(2 * y + oc)
    dyp = dev_row(2 * yp + c)
    dym = dev_row(2 * ym + c)

    def remote(src, dst, ss, rs, dev):
        return pltpu.make_async_remote_copy(
            src_ref=src, dst_ref=dst, send_sem=ss, recv_sem=rs, device_id=dev, device_id_type=MESH
        )

    barrier = pltpu.get_barrier_semaphore()
    peers = [sib, dyp, dym]
    peers += [dev_x((x + d) % NX) for d in X_ORDER]
    peers += [dev_z((z + d) % NZ) for d in Z_ORDER]
    for p in peers:
        pl.semaphore_signal(barrier, inc=1, device_id=p, device_id_type=MESH)

    w[...] = (coeffs[...].astype(jnp.float32) * occ[...]).astype(jnp.bfloat16)
    mx[x] = meta[...]
    pl.semaphore_wait(barrier, len(peers))

    pending = []
    g_p = remote(coeffs, f_a, g_send.at[0], g_recv.at[0], dyp)
    g_p.start()
    g_s = remote(coeffs, b0, g_send.at[1], g_recv.at[1], sib)
    g_s.start()
    m_x = [
        remote(mx.at[x], mx.at[x], m_send.at[d], m_recv.at[d], dev_x((x + d) % NX)) for d in X_ORDER
    ]
    for m in m_x:
        m.start()

    def compute_tiles(panel, k, j, s):
        def one(p, carry):
            a = w[left[s, p]]
            b = panel[right[s, p]]
            t = lax.dot_general(
                a, b, (((1,), (1,)), ((), ())), preferred_element_type=jnp.float32
            )
            tiles[k, p // 4, (p // 2) % 2, j, p % 2] = t.astype(jnp.bfloat16)
            return carry

        lax.fori_loop(0, NTP, one, 0)

    x1 = {}
    x2c = {}
    zc = {}
    e1c = {}
    e2c = {}

    def x1_start(k):
        x1[k] = (
            remote(tiles.at[k, x2, 0], x1_l.at[k], x_send.at[k, 0], x_recv.at[k, 0], dev_x(xr)),
            remote(tiles.at[k, x2, 1], x1_r.at[k], x_send.at[k, 1], x_recv.at[k, 1], dev_x(xl)),
        )
        for q in x1[k]:
            q.start()

    def x2_start(k):
        to_r = remote(tiles.at[k, xr], x2_l.at[k], x_send.at[k, 2], x_recv.at[k, 2], dev_x(xr))
        to_l = remote(tiles.at[k, xl], x2_r.at[k], x_send.at[k, 3], x_recv.at[k, 3], dev_x(xl))
        for half, dst, first, second in ((0, xr, x1[k][0], to_r), (1, xl, x1[k][1], to_l)):
            first.wait_recv()
            got = (x1_l, x1_r)[half]
            tiles[k, dst, half] = (
                tiles[k, dst, half].astype(jnp.float32) + got[k].astype(jnp.float32)
            ).astype(jnp.bfloat16)
            second.start()
        x2c[k] = (to_r, to_l)

    def z_start(k):
        for q in x2c[k]:
            q.wait_recv()
        for j in range(2):
            for h in range(2):
                total = (
                    tiles[k, x, h, j].astype(jnp.float32)
                    + x2_l[k, h, j].astype(jnp.float32)
                    + x2_r[k, h, j].astype(jnp.float32)
                )
                zs[k, pl.ds(4 * j + 2 * h, 2)] = total.astype(jnp.bfloat16)
        cs = []
        for d in Z_ORDER:
            to = (z + d) % NZ
            q = remote(zs.at[k, to], rz.at[k, z], z_send.at[k, d], z_recv.at[k, d], dev_z(to))
            q.start()
            cs.append(q)
        rz[k, z] = zs[k, z]
        zc[k] = cs

    sj = z // 4
    si = z % 4

    def panel_of(k, j):
        if k == 0:
            a, b = 2 * y + c, 2 * y + oc
        elif k == 1:
            a, b = 2 * ym + c, 2 * yp + oc
        elif k == 2:
            a, b = 2 * yp + c, 2 * ym + oc
        else:
            a, b = 2 * y2 + c, 2 * y2 + oc
        return a if j == 0 else b

    def my_panel(k):
        return panel_of(k, 0) * (1 - sj) + panel_of(k, 1) * sj

    def collocate(k):
        for q in zc[k]:
            q.wait_recv()
        block = jnp.sum(rz[k].astype(jnp.float32), axis=0).astype(jnp.bfloat16)
        s = my_panel(k)
        p = 4 * x + si
        same = jnp.logical_and(s == r, left[s, p] == right[s, p])
        scale = jnp.where(same, 1.0, 2.0).astype(jnp.float32)

        def one(t, carry):
            pa = meta_s[k, si, 12 + t]
            pb = meta_s[k, si, 18 + t]
            for ch in range(G // CHUNK):
                cols = pl.ds(ch * CHUNK, CHUNK)
                prod = jnp.dot(block, basis[pb, :, cols], preferred_element_type=jnp.float32)
                row = jnp.sum(basis[pa, :, cols].astype(jnp.float32) * prod, axis=0, keepdims=True)
                row = row * scale
                for q in range(CHUNK // GL):
                    terms[k, t, pl.ds(ch * (CHUNK // GL) + q, 1), :] = row[:, q * GL : (q + 1) * GL]
            return carry

        lax.fori_loop(0, TOP, one, 0)
        vals = [terms[k, t] for t in range(TOP)]
        own = [meta_s[k, si, t] for t in range(TOP)]

        def place(o, carry):
            acc = jnp.zeros((GS, GL), jnp.float32)
            for t in range(TOP):
                acc = jnp.where(own[t] == o, vals[t], acc)
            send_e[k, o % NX, o // NX] = acc.astype(jnp.bfloat16)
            return carry

        lax.fori_loop(0, NX * NZ, place, 0)
        cs = []
        for d in X_ORDER:
            to = (x + d) % NX
            q = remote(send_e.at[k, to], e1.at[k, x], e_send.at[k, d], e_recv.at[k, d], dev_x(to))
            q.start()
            cs.append(q)
        e1[k, x] = send_e[k, x]
        e1c[k] = cs

    def e2_start(k):
        for q in e1c[k]:
            q.wait_recv()
        cs = []
        for d in Z_ORDER:
            to = (z + d) % NZ
            q = remote(
                e1.at[k, :, to], arr.at[k, z], e_send.at[k, 4 + d], e_recv.at[k, 4 + d], dev_z(to)
            )
            q.start()
            cs.append(q)
        arr[k, z] = e1[k, :, z]
        e2c[k] = cs

    def finish(k, acc):
        for q in e2c[k]:
            q.wait_recv()

        def one(i, acc):
            zf, xf = i // NX, i % NX
            jj = zf // 4
            ii = zf % 4
            s = panel_of(k, 0) * (1 - jj) + panel_of(k, 1) * jj
            val = arr[k, zf, xf].astype(jnp.float32)
            slot = hits[s, xf, pl.ds(ii, 1), :]
            return tuple(acc[b] + jnp.where(slot == float(b), val, 0.0) for b in range(NBR))

        return lax.fori_loop(0, NX * NZ, one, acc)

    compute_tiles(coeffs, 0, 0, panel_of(0, 0))
    for m in m_x:
        m.wait_recv()
    m_z = []
    for d in Z_ORDER:
        to = (z + d) % NZ
        q = remote(mx, mz.at[z], m_send.at[4 + d], m_recv.at[4 + d], dev_z(to))
        q.start()
        m_z.append(q)
    mz[z] = mx[...]
    g_s.wait_recv()
    compute_tiles(b0, 0, 1, panel_of(0, 1))
    x1_start(0)
    for q in m_z:
        q.wait_recv()
    locals_ = []
    for k in range(4):
        q = pltpu.make_async_copy(mz.at[my_panel(k), x], meta_s.at[k], l_sem.at[k])
        q.start()
        locals_.append(q)

    lane = lax.broadcasted_iota(jnp.int32, (8, 128), 1)

    def hit(i, carry):
        zf, xf = i // NX, i % NX
        m = mz[zf, xf]
        slots = pltpu.roll(m, 128 - TOP, axis=1)
        mine = jnp.logical_and(lane < TOP, m == band)
        val = jnp.where(mine, slots + 1, 0).astype(jnp.float32)
        hits[zf, xf] = jnp.broadcast_to(jnp.sum(val, axis=1, keepdims=True) - 1.0, (8, 128))
        return carry

    lax.fori_loop(0, NX * NZ, hit, 0)
    for q in locals_:
        q.wait()
    x2_start(0)
    g_p.wait_send()
    g_m = remote(coeffs, s_a, g_send.at[2], g_recv.at[2], dym)
    g_m.start()

    g_p.wait_recv()
    g_fs = remote(f_a, f_b, g_send.at[3], g_recv.at[3], sib)
    g_fs.start()
    top = pl.ds(0, BLOCKS // 2)
    low = pl.ds(BLOCKS // 2, BLOCKS // 2)
    g_f = remote(f_a.at[top], t_a.at[top], g_send.at[4], g_recv.at[4], dyp)
    g_f.start()
    compute_tiles(f_a, 1, 0, panel_of(1, 0))
    z_start(0)
    g_fs.wait_recv()
    compute_tiles(f_b, 1, 1, panel_of(1, 1))
    x1_start(1)

    g_m.wait_recv()
    g_ms = remote(s_a, s_b, g_send.at[5], g_recv.at[5], sib)
    g_ms.start()
    g_b = remote(s_a.at[low], t_a.at[low], g_send.at[6], g_recv.at[6], dym)
    g_b.start()
    x2_start(1)
    compute_tiles(s_a, 2, 0, panel_of(2, 0))
    g_ms.wait_recv()
    compute_tiles(s_b, 2, 1, panel_of(2, 1))
    x1_start(2)
    z_start(1)
    collocate(0)

    g_f.wait_recv()
    g_b.wait_recv()
    g_ts = remote(t_a, t_b, g_send.at[7], g_recv.at[7], sib)
    g_ts.start()
    x2_start(2)
    compute_tiles(t_a, 3, 0, panel_of(3, 0))
    g_ts.wait_recv()
    compute_tiles(t_b, 3, 1, panel_of(3, 1))
    x1_start(3)
    z_start(2)
    e2_start(0)
    collocate(1)
    x2_start(3)
    e2_start(1)
    collocate(2)
    z_start(3)
    e2_start(2)
    acc = tuple(jnp.zeros((GS, GL), jnp.float32) for _ in range(NBR))
    acc = finish(0, acc)
    collocate(3)
    e2_start(3)
    acc = finish(1, acc)
    acc = finish(2, acc)
    acc = finish(3, acc)
    for b in range(NBR):
        out[b] = acc[b]

    pending += [g_p, g_s, g_m, g_fs, g_f, g_ms, g_b, g_ts] + m_x + m_z
    for k in range(4):
        pending += list(x1[k]) + list(x2c[k]) + zc[k] + e1c[k] + e2c[k]
    for q in pending:
        if q is not g_p:
            q.wait_send()


def body(coeffs, occupation, tile_left, tile_right, owners, brick_slot, patterns, basis_table):
    meta = jnp.concatenate([owners, brick_slot, patterns[:, :, 0], patterns[:, :, 1]], axis=1)
    meta = jnp.pad(meta, ((0, 4), (0, 128 - 4 * TOP)))
    vm = pl.BlockSpec(memory_space=pltpu.VMEM)
    sm = pl.BlockSpec(memory_space=pltpu.SMEM)
    bf, f32 = jnp.bfloat16, jnp.float32
    panel = pltpu.VMEM((BLOCKS, BS, KD), bf)
    out = pl.pallas_call(
        kernel,
        out_shape=jax.ShapeDtypeStruct((NBR, GS, GL), f32),
        in_specs=[vm, vm, sm, sm, vm, vm],
        out_specs=vm,
        scratch_shapes=[panel] * 8
        + [
            pltpu.VMEM((4, NX, 2, 2, 2, BS, BS), bf),
            pltpu.VMEM((4, 2, 2, BS, BS), bf),
            pltpu.VMEM((4, 2, 2, BS, BS), bf),
            pltpu.VMEM((4, 2, 2, 2, BS, BS), bf),
            pltpu.VMEM((4, 2, 2, 2, BS, BS), bf),
            pltpu.VMEM((4, NZ, BS, BS), bf),
            pltpu.VMEM((4, NZ, BS, BS), bf),
            pltpu.VMEM((4, TOP, GS, GL), f32),
            pltpu.VMEM((4, NX, NZ, GS, GL), bf),
            pltpu.VMEM((4, NX, NZ, GS, GL), bf),
            pltpu.VMEM((4, NZ, NX, GS, GL), bf),
            pltpu.VMEM((NX, 8, 128), jnp.int32),
            pltpu.VMEM((NZ, NX, 8, 128), jnp.int32),
            pltpu.VMEM((NZ, NX, 8, 128), f32),
            pltpu.SMEM((4, 8, 128), jnp.int32),
            pltpu.SemaphoreType.DMA((8,)),
            pltpu.SemaphoreType.DMA((8,)),
            pltpu.SemaphoreType.DMA((4, 4)),
            pltpu.SemaphoreType.DMA((4, 4)),
            pltpu.SemaphoreType.DMA((4, NZ)),
            pltpu.SemaphoreType.DMA((4, NZ)),
            pltpu.SemaphoreType.DMA((4, 12)),
            pltpu.SemaphoreType.DMA((4, 12)),
            pltpu.SemaphoreType.DMA((12,)),
            pltpu.SemaphoreType.DMA((12,)),
            pltpu.SemaphoreType.DMA((4,)),
        ],
        compiler_params=pltpu.CompilerParams(
            collective_id=0, has_side_effects=True, vmem_limit_bytes=50 * 1024 * 1024
        ),
        cost_estimate=pl.CostEstimate(
            flops=4 * 10**9, bytes_accessed=4 * 10**6, transcendentals=0
        ),
    )(
        coeffs.reshape(BLOCKS, BS, KD),
        occupation.reshape(1, KD),
        tile_left[0],
        tile_right[0],
        meta,
        basis_table,
    )
    return out.reshape(NBR, G)


def solution(mesh):
    return jax.shard_map(
        body,
        mesh=mesh,
        in_specs=(
            P("row", "band"),
            P("band"),
            P("row", None, None),
            P("row", None, None),
            P(("row", "band"), None),
            P(("row", "band"), None),
            P(("row", "band"), None, None),
            P(),
        ),
        out_specs=P(("row", "band"), None),
        check_vma=False,
    )
```

time: 537 us -> 102 us (0.19)
  waiting for transfers between devices: 303 us -> 0 us
  local copies, waits for them, and re-layouts: 119 us -> 6.29 us
  Pallas kernels: 0 us -> 94.4 us
  matrix products: 74.3 us -> 0 us
  starting transfers between devices: 18.1 us -> 0 us
  between operations: 13.6 us -> 0.02 us
    reduce_scatter x1 -> x0, waiting for transfers between devices: 203 us -> none  [body(): lax.psum_scatter(flat, 'band', scatter_dimension=0, tiled=True)]
    gather x52 -> x0, local copies, waits for them, and re-layouts: 98.9 us -> none  [the longest x16 32.1 us: one_group(): basis_table[group_right]]
    pallas_call x0 -> x1, Pallas kernels: none -> 94.4 us  [body(): pl.pallas_call(kernel, out_shape=jax.ShapeDtypeStruct((NBR, GS, GL), f32)...]
    dot_general x26 -> x0, matrix products: 74.3 us -> none  [the longest x16 47.6 us: collocate(): jnp.einsum('sij,sjg->sig', blocks, right_rows, preferred_element_type=jnp...]
    all_gather x1 -> x0, waiting for transfers between devices: 54.4 us -> none  [body(): piece = lax.all_gather(coeffs, 'row', axis=0, tiled=True)]
    all_to_all x2 -> x0, waiting for transfers between devices: 44.2 us -> none  [the longest x1 44.2 us: body(): lax.all_to_all(outgoing.reshape(band_count, capacity, BS * BS), 'band', s...]
    all_to_all x2 -> x0, starting transfers between devices: 18.1 us -> none  [the longest x1 10.1 us: body(): lax.all_to_all(outgoing_details.reshape(band_count, capacity, 4), 'band',...]
    squeeze x8 -> x0, local copies, waits for them, and re-layouts: 10.6 us -> none  [one_panel(): rows_right = pieces[index][right_table[index]]]
  transfers between devices with their start and end apart: 4 -> 0, of which waited for: 3 -> 0; matrix products, arithmetic and copies ran while one was open for 3% -> 0% of each run, Pallas kernels for 0% -> 0%
where the time goes in v1:
time: 102 us
  Pallas kernels  94.4 us (93%)
  local copies, waits for them, and re-layouts  6.29 us (6%)
    pallas_call x1, Pallas kernels, body(): pl.pallas_call(kernel, out_shape=jax.ShapeDtypeStruct((NBR, GS, GL), f32)...  94.4 us
    unnamed x11, local copies, waits for them, and re-layouts  5.52 us

profile of v1, /device:TPU:32, one launch (start us, length us, event | category | flops | bytes accessed | tf_op | source)
XLA Modules:
  0.0 101.5 jit_solution(9387739351496747440)
XLA Ops:
  0.0 0.8 fusion
  0.8 0.8 pad_add_fusion
  1.5 0.0 copy-start
  1.6 1.6 %copy-done = bf16[4,128,2048]{2,1,0:T(8,128)(2,1)S(1)} copy-done((bf16[4,128,2048]{2,1,0:T(8,128)(2,1)S(1)}, bf16[4,128,2048]{2,1,0:T(8,128)(2,1)}, u32[]{:S(2)}) %copy-start) | copy-done | bytes 2097176
  3.1 0.0 copy-start.1
  3.1 1.2 %copy-done.1 = bf16[1024,512]{1,0:T(8,128)(2,1)S(1)} copy-done((bf16[1024,512]{1,0:T(8,128)(2,1)S(1)}, bf16[1024,512]{1,0:T(8,128)(2,1)}, u32[]{:S(2)}) %copy-start.1) | copy-done | bytes 1048600
  4.4 0.0 copy-start.2
  4.4 0.7 copy-done.2
  5.1 0.0 copy-start.3
  5.1 0.7 copy-done.3
  5.7 0.0 copy-start.4
  5.7 0.7 copy-done.4
  6.4 94.4 %shard_map.82 = f32[8,16,128]{2,1,0:T(8,128)S(1)} custom-call(bf16[8,128,512]{2,1,0:T(8,128)(2,1)S(1)} %bitcast.11, f32[1,512]{1,0:T(1,128)S(1)} %bitcast.14, s32[8,16]{1,0:T(8,128)S(1)} %bitcast.12, s32[8,16]{1,0:T(8,128)S(1)} %bitcast.13, s32[8,128]{1,0:T(8,128)S(1)} %pad.4.meta, bf16[4,128,2048]{2,1,0:T(8,128)(2,1)S(1)} %copy-done), custom_call_target="tpu_custom_call" | custom-call | flops 4000000000 | bytes 4000000 | tf_op jit(solution)/shard_map/pallas_call | solution.py:371
  100.9 0.7 copy.11
  (1 shorter events, 0.0 us)
Async XLA Ops:
  1.5 1.6 %copy-start = (bf16[4,128,2048]{2,1,0:T(8,128)(2,1)S(1)}, bf16[4,128,2048]{2,1,0:T(8,128)(2,1)}, u32[]{:S(2)}) copy-start(bf16[4,128,2048]{2,1,0:T(8,128)(2,1)} %basis.1) | copy-start | bytes 6291460
  3.1 1.2 %copy-start.1 = (bf16[1024,512]{1,0:T(8,128)(2,1)S(1)}, bf16[1024,512]{1,0:T(8,128)(2,1)}, u32[]{:S(2)}) copy-start(bf16[1024,512]{1,0:T(8,128)(2,1)} %param.8) | copy-start | bytes 3145732
  4.4 0.7 copy-start.2
  5.1 0.7 copy-start.3
  5.7 0.7 copy-start.4

commit v2 on v1

v2 whole, which is shorter than its diff:
```python
import jax
import jax.numpy as jnp
from jax import lax
from jax.experimental import pallas as pl
from jax.experimental.pallas import tpu as pltpu
from jax.sharding import PartitionSpec as P

BS = 128
NBR = 8
TOP = 6
G = 2048
GS, GL = 16, 128
NTP = 16
BLOCKS = 8
KD = 512
NX, NY, NZ = 4, 4, 8
CHUNK = 512
Z_ORDER = (4, 3, 5, 2, 6, 1, 7)
X_ORDER = (2, 1, 3)
E_ORDER = tuple(zz * NX + xx for zz in Z_ORDER + (0,) for xx in (2, 1, 3, 0) if zz or xx)
VMEM = 62 * 2**20
MESH = pl.DeviceIdType.MESH


def kernel(
    coeffs_hbm,
    occ_hbm,
    left_hbm,
    right_hbm,
    meta_hbm,
    basis_hbm,
    out,
    coeffs,
    occ,
    basis,
    w,
    b0,
    f_a,
    f_b,
    s_a,
    s_b,
    t_a,
    t_b,
    tiles,
    x1_l,
    x1_r,
    x2_l,
    x2_r,
    zs,
    rz,
    terms,
    send_e,
    arr,
    mx,
    mz,
    hits,
    meta_s,
    left_s,
    right_s,
    g_send,
    g_recv,
    x_send,
    x_recv,
    z_send,
    z_recv,
    e_send,
    e_recv,
    m_send,
    m_recv,
    l_sem,
    i_sem,
):
    r = lax.axis_index("row")
    band = lax.axis_index("band")
    y, c = r // 2, r % 2
    z, x = band // NX, band % NX
    sg = 1 - 2 * c
    yp, ym, y2 = (y + sg + NY) % NY, (y - sg + NY) % NY, (y + 2) % NY
    oc = 1 - c
    xr, xl, x2 = (x + 1) % NX, (x + 3) % NX, (x + 2) % NX

    def dev_row(rr):
        return (rr, band)

    def dev_x(xx):
        return (r, z * NX + xx)

    def dev_at(zz, xx):
        return (r, zz * NX + xx)

    def dev_z(zz):
        return (r, zz * NX + x)

    sib = dev_row(2 * y + oc)
    dyp = dev_row(2 * yp + c)
    dym = dev_row(2 * ym + c)

    def remote(src, dst, ss, rs, dev):
        return pltpu.make_async_remote_copy(
            src_ref=src, dst_ref=dst, send_sem=ss, recv_sem=rs, device_id=dev, device_id_type=MESH
        )

    barrier = pltpu.get_barrier_semaphore()
    peers = [sib, dyp, dym]
    peers += [dev_at((z + d // NX) % NZ, (x + d) % NX) for d in range(1, NX * NZ)]
    for p in peers:
        pl.semaphore_signal(barrier, inc=1, device_id=p, device_id_type=MESH)

    loads = [
        pltpu.make_async_copy(src, dst, i_sem.at[i])
        for i, (src, dst) in enumerate(
            (
                (coeffs_hbm, coeffs),
                (occ_hbm, occ),
                (left_hbm, left_s),
                (right_hbm, right_s),
                (meta_hbm, mx.at[x]),
                (basis_hbm, basis),
            )
        )
    ]
    for q in loads:
        q.start()
    for q in loads[:5]:
        q.wait()
    w[...] = (coeffs[...].astype(jnp.float32) * occ[...]).astype(jnp.bfloat16)
    pl.semaphore_wait(barrier, len(peers))

    pending = []
    halves = (pl.ds(0, BLOCKS // 2), pl.ds(BLOCKS // 2, BLOCKS // 2))
    g_s = remote(coeffs_hbm, b0, g_send.at[0], g_recv.at[0], sib)
    g_p = [
        remote(coeffs_hbm.at[v], f_a.at[v], g_send.at[1 + i], g_recv.at[1 + i], dyp)
        for i, v in enumerate(halves)
    ]
    g_m = [
        remote(coeffs_hbm.at[v], s_a.at[v], g_send.at[3 + i], g_recv.at[3 + i], dym)
        for i, v in enumerate(halves)
    ]
    m_x = [
        remote(mx.at[x], mx.at[x], m_send.at[d], m_recv.at[d], dev_x((x + d) % NX)) for d in X_ORDER
    ]
    g_s.start()
    for q in g_p + m_x:
        q.start()

    def compute_tiles(panel, h, s):
        def one(p, carry):
            a = w[left_s[0, s, p]]
            b = panel[right_s[0, s, p]]
            t = lax.dot_general(
                a, b, (((1,), (1,)), ((), ())), preferred_element_type=jnp.float32
            )
            tiles[h, p // 4, p % 4] = t.astype(jnp.bfloat16)
            return carry

        lax.fori_loop(0, NTP, one, 0)

    x1 = {}
    x2c = {}
    top, low = pl.ds(0, 2), pl.ds(2, 2)

    def x1_start(h):
        x1[h] = (
            remote(tiles.at[h, x2, top], x1_l.at[h], x_send.at[h, 0], x_recv.at[h, 0], dev_x(xr)),
            remote(tiles.at[h, x2, low], x1_r.at[h], x_send.at[h, 1], x_recv.at[h, 1], dev_x(xl)),
        )
        for q in x1[h]:
            q.start()

    def x2_start(h):
        to_r = remote(tiles.at[h, xr], x2_l.at[h], x_send.at[h, 2], x_recv.at[h, 2], dev_x(xr))
        to_l = remote(tiles.at[h, xl], x2_r.at[h], x_send.at[h, 3], x_recv.at[h, 3], dev_x(xl))
        for part, dst, got, first, second in (
            (top, xr, x1_l, x1[h][0], to_r),
            (low, xl, x1_r, x1[h][1], to_l),
        ):
            first.wait_recv()
            tiles[h, dst, part] = (
                tiles[h, dst, part].astype(jnp.float32) + got[h].astype(jnp.float32)
            ).astype(jnp.bfloat16)
            second.start()
        x2c[h] = (to_r, to_l)

    def z_copy(h, i):
        to = 4 * (h % 2) + i
        return remote(
            zs.at[h, i], rz.at[h // 2, z], z_send.at[h, i], z_recv.at[h // 2, z], dev_z(to)
        )

    def z_start(h):
        for q in x2c[h]:
            q.wait_recv()
        for i in range(4):
            total = (
                tiles[h, x, i].astype(jnp.float32)
                + x2_l[h, i].astype(jnp.float32)
                + x2_r[h, i].astype(jnp.float32)
            ).astype(jnp.bfloat16)
            zs[h, i] = total
            to = 4 * (h % 2) + i

            @pl.when(z != to)
            def _():
                z_copy(h, i).start()

            @pl.when(z == to)
            def _():
                rz[h // 2, z] = total

    def z_drain(h):
        for i in range(4):

            @pl.when(z != 4 * (h % 2) + i)
            def _():
                z_copy(h, i).wait_send()

    sj = z // 4
    si = z % 4

    def panel_of(k, j):
        if k == 0:
            a, b = 2 * y + c, 2 * y + oc
        elif k == 1:
            a, b = 2 * ym + c, 2 * yp + oc
        elif k == 2:
            a, b = 2 * yp + c, 2 * ym + oc
        else:
            a, b = 2 * y2 + c, 2 * y2 + oc
        return a if j == 0 else b

    def my_panel(k):
        return panel_of(k, 0) * (1 - sj) + panel_of(k, 1) * sj

    def collocate(k):
        for zf in range(NZ):

            @pl.when(z != zf)
            def _():
                remote(
                    rz.at[k, zf], rz.at[k, zf], z_send.at[0, 0], z_recv.at[k, zf], dev_z(zf)
                ).wait_recv()

        block = jnp.sum(rz[k].astype(jnp.float32), axis=0).astype(jnp.bfloat16)
        s = my_panel(k)
        p = 4 * x + si
        same = jnp.logical_and(s == r, left_s[0, s, p] == right_s[0, s, p])
        scale = jnp.where(same, 1.0, 2.0).astype(jnp.float32)

        def one(t, carry):
            pa = meta_s[k, 2 * si, 12 + t]
            pb = meta_s[k, 2 * si + 1, 12 + t]
            for ch in range(G // CHUNK):
                cols = pl.ds(ch * CHUNK, CHUNK)
                prod = jnp.dot(block, basis[pb, :, cols], preferred_element_type=jnp.float32)
                row = jnp.sum(basis[pa, :, cols].astype(jnp.float32) * prod, axis=0, keepdims=True)
                row = row * scale
                for q in range(CHUNK // GL):
                    terms[k, t, pl.ds(ch * (CHUNK // GL) + q, 1), :] = row[:, q * GL : (q + 1) * GL]
            return carry

        lax.fori_loop(0, TOP, one, 0)
        vals = [terms[k, t] for t in range(TOP)]
        own = [meta_s[k, si, t] for t in range(TOP)]

        def place(o, carry):
            acc = jnp.zeros((GS, GL), jnp.float32)
            for t in range(TOP):
                acc = jnp.where(own[t] == o, vals[t], acc)
            send_e[k, o] = acc.astype(jnp.bfloat16)
            return carry

        lax.fori_loop(0, NX * NZ, place, 0)
        for d in E_ORDER:
            e_copy(k, d).start()
        arr[k, band] = send_e[k, band]

    def e_copy(k, d):
        zz, xx = (z + d // NX) % NZ, (x + d) % NX
        return remote(
            send_e.at[k, zz * NX + xx],
            arr.at[k, band],
            e_send.at[k],
            e_recv.at[k],
            dev_at(zz, xx),
        )

    def e_all(k):
        others = pl.ds(0, NX * NZ - 1)
        return remote(send_e.at[k, others], arr.at[k, others], e_send.at[k], e_recv.at[k], sib)

    def finish(k, acc):
        e_all(k).wait_recv()

        def one(i, acc):
            zf, xf = i // NX, i % NX
            jj = zf // 4
            ii = zf % 4
            s = panel_of(k, 0) * (1 - jj) + panel_of(k, 1) * jj
            val = arr[k, i].astype(jnp.float32)
            slot = hits[s * NX + xf, pl.ds(ii, 1), :]
            return tuple(acc[b] + jnp.where(slot == float(b), val, 0.0) for b in range(NBR))

        return lax.fori_loop(0, NX * NZ, one, acc)

    def to_sibling(src, dst, i, at):
        q = remote(src.at[halves[i]], dst.at[halves[i]], g_send.at[at], g_recv.at[at], sib)
        q.start()
        return q

    compute_tiles(coeffs, 0, panel_of(0, 0))
    x1_start(0)
    for m in m_x:
        m.wait_recv()
    m_z = []
    for d in Z_ORDER:
        to = (z + d) % NZ
        q = remote(mx, mz.at[z], m_send.at[4 + d], m_recv.at[4 + d], dev_z(to))
        q.start()
        m_z.append(q)
    mz[z] = mx[...]
    g_s.wait_recv()
    compute_tiles(b0, 1, panel_of(0, 1))
    x1_start(1)
    x2_start(0)
    g_p[0].wait_recv()
    for q in g_m:
        q.start()
    g_fs = [to_sibling(f_a, f_b, 0, 5)]
    x2_start(1)
    for q in m_z:
        q.wait_recv()
    locals_ = []
    for k in range(4):
        q = pltpu.make_async_copy(mz.at[my_panel(k), x], meta_s.at[k], l_sem.at[k])
        q.start()
        locals_.append(q)
    lane = lax.broadcasted_iota(jnp.int32, (NX * NZ, 8, 128), 2)
    every = mz[...].reshape(NX * NZ, 8, 128)
    slots = pltpu.roll(every, 128 - TOP, axis=2)
    mine = jnp.logical_and(lane < TOP, every == band)
    found = jnp.where(mine, slots + 1, 0).astype(jnp.bfloat16).reshape(NX * NZ * 8, 128)
    ones = jnp.ones((128, 128), jnp.bfloat16)
    found = jnp.dot(found, ones, preferred_element_type=jnp.float32) - 1.0
    hits[...] = found.reshape(NX * NZ, 8, 128)

    g_p[1].wait_recv()
    g_fs.append(to_sibling(f_a, f_b, 1, 6))
    compute_tiles(f_a, 2, panel_of(1, 0))
    x1_start(2)
    z_start(0)
    for q in g_fs:
        q.wait_recv()
    compute_tiles(f_b, 3, panel_of(1, 1))
    x1_start(3)
    g_m[0].wait_recv()
    g_f = [
        remote(f_a.at[v], t_a.at[v], g_send.at[7 + i], g_recv.at[7 + i], dyp)
        for i, v in enumerate(halves)
    ]
    for q in g_f:
        q.start()
    g_ms = [to_sibling(s_a, s_b, 0, 9)]
    z_start(1)
    x2_start(2)
    x2_start(3)
    for q in locals_:
        q.wait()
    loads[5].wait()

    g_m[1].wait_recv()
    g_ms.append(to_sibling(s_a, s_b, 1, 10))
    compute_tiles(s_a, 4, panel_of(2, 0))
    x1_start(4)
    z_start(2)
    for q in g_ms:
        q.wait_recv()
    compute_tiles(s_b, 5, panel_of(2, 1))
    x1_start(5)
    g_f[0].wait_recv()
    g_ts = [to_sibling(t_a, t_b, 0, 11)]
    z_start(3)
    x2_start(4)
    collocate(0)
    x2_start(5)

    g_f[1].wait_recv()
    g_ts.append(to_sibling(t_a, t_b, 1, 12))
    compute_tiles(t_a, 6, panel_of(3, 0))
    x1_start(6)
    z_start(4)
    for q in g_ts:
        q.wait_recv()
    compute_tiles(t_b, 7, panel_of(3, 1))
    x1_start(7)
    z_start(5)
    x2_start(6)
    x2_start(7)
    collocate(1)
    z_start(6)
    z_start(7)
    collocate(2)
    acc = tuple(jnp.zeros((GS, GL), jnp.float32) for _ in range(NBR))
    acc = finish(0, acc)
    acc = finish(1, acc)
    collocate(3)
    acc = finish(2, acc)
    acc = finish(3, acc)
    for b in range(NBR):
        for q in range(GS):
            out[pl.ds(b, 1), pl.ds(q * GL, GL)] = acc[b][q : q + 1, :]

    pending += [g_s] + g_p + g_m + g_fs + g_f + g_ms + g_ts + m_x + m_z
    for h in range(8):
        pending += list(x1[h]) + list(x2c[h])
    for q in pending:
        q.wait_send()
    for h in range(8):
        z_drain(h)
    for k in range(4):
        e_all(k).wait_send()


def body(coeffs, occupation, tile_left, tile_right, owners, brick_slot, patterns, basis_table):
    def place(a, at):
        return jnp.pad(a, ((0, 8 - a.shape[0]), (at, 128 - TOP - at)))

    meta = (
        place(owners, 0)
        + place(brick_slot, TOP)
        + place(jnp.transpose(patterns, (0, 2, 1)).reshape(8, TOP), 2 * TOP)
    )
    hbm = pl.BlockSpec(memory_space=pltpu.HBM)
    bf, f32 = jnp.bfloat16, jnp.float32
    panel = pltpu.VMEM((BLOCKS, BS, KD), bf)
    dma = pltpu.SemaphoreType.DMA
    out = pl.pallas_call(
        kernel,
        out_shape=jax.ShapeDtypeStruct((NBR, G), f32),
        in_specs=[hbm] * 6,
        out_specs=pl.BlockSpec(memory_space=pltpu.VMEM),
        scratch_shapes=[
            panel,
            pltpu.VMEM((1, KD), f32),
            pltpu.VMEM((4, BS, G), bf),
        ]
        + [panel] * 8
        + [
            pltpu.VMEM((8, NX, 4, BS, BS), bf),
            pltpu.VMEM((8, 2, BS, BS), bf),
            pltpu.VMEM((8, 2, BS, BS), bf),
            pltpu.VMEM((8, 4, BS, BS), bf),
            pltpu.VMEM((8, 4, BS, BS), bf),
            pltpu.VMEM((8, 4, BS, BS), bf),
            pltpu.VMEM((4, NZ, BS, BS), bf),
            pltpu.VMEM((4, TOP, GS, GL), f32),
            pltpu.VMEM((4, NX * NZ, GS, GL), bf),
            pltpu.VMEM((4, NX * NZ, GS, GL), bf),
            pltpu.VMEM((NX, 8, 128), jnp.int32),
            pltpu.VMEM((NZ, NX, 8, 128), jnp.int32),
            pltpu.VMEM((NX * NZ, 8, 128), f32),
            pltpu.SMEM((4, 8, 128), jnp.int32),
            pltpu.SMEM((1, 8, NTP), jnp.int32),
            pltpu.SMEM((1, 8, NTP), jnp.int32),
            dma((13,)),
            dma((13,)),
            dma((8, 4)),
            dma((8, 4)),
            dma((8, 4)),
            dma((4, NZ)),
            dma((4,)),
            dma((4,)),
            dma((12,)),
            dma((12,)),
            dma((4,)),
            dma((6,)),
        ],
        compiler_params=pltpu.CompilerParams(
            collective_id=0, has_side_effects=True, vmem_limit_bytes=VMEM
        ),
        cost_estimate=pl.CostEstimate(
            flops=4 * 10**9, bytes_accessed=4 * 10**6, transcendentals=0
        ),
    )(
        coeffs.reshape(BLOCKS, BS, KD),
        occupation.reshape(1, KD),
        tile_left,
        tile_right,
        meta,
        basis_table,
    )
    return out


def solution(mesh):
    return jax.shard_map(
        body,
        mesh=mesh,
        in_specs=(
            P("row", "band"),
            P("band"),
            P("row", None, None),
            P("row", None, None),
            P(("row", "band"), None),
            P(("row", "band"), None),
            P(("row", "band"), None, None),
            P(),
        ),
        out_specs=P(("row", "band"), None),
        check_vma=False,
    )
```

time: 102 us -> 92.2 us (0.904)
  Pallas kernels: 94.4 us -> 89.2 us
  local copies, waits for them, and re-layouts: 6.29 us -> 1.47 us
    pallas_call x1, Pallas kernels: 94.4 us -> 89.2 us  [body(): pl.pallas_call(kernel, out_shape=jax.ShapeDtypeStruct((NBR, G), f32), in_...]
    unnamed x11 -> x1, local copies, waits for them, and re-layouts: 5.52 us -> 1.47 us
    add x0 -> x1, other arithmetic: none -> 1.38 us  [body(): place(owners, 0) + place(brick_slot, TOP)]
where the time goes in v2:
time: 92.2 us; the launch traced here: 92.1 us
  Pallas kernels  89.2 us (97%)
  local copies, waits for them, and re-layouts  1.47 us (2%)
  other arithmetic  1.38 us (1%)
    pallas_call x1, Pallas kernels, body(): pl.pallas_call(kernel, out_shape=jax.ShapeDtypeStruct((NBR, G), f32), in_...  89.2 us

profile of v2, /device:TPU:32, one launch (start us, length us, event | category | flops | bytes accessed | tf_op | source)
XLA Modules:
  0.0 92.1 jit_solution(10391494545853937588)
XLA Ops:
  0.0 1.4 %pad_add_fusion.meta_hbm = s32[8,128]{1,0:T(8,128)} fusion(s32[8,6]{1,0:T(8,128)} %bitcast.5, s32[4,6]{1,0:T(4,128)} %param.13, s32[4,6]{1,0:T(4,128)} %param.12), kind=kLoop, calls=%fused_computation | loop fusion | flops 2048 | bytes 4480 | tf_op jit(solution)/shard_map/add | solution.py:429
  1.4 89.2 %shard_map.82 = f32[8,2048]{1,0:T(8,128)} custom-call(bf16[8,128,512]{2,1,0:T(8,128)(2,1)} %bitcast.6, f32[1,512]{1,0:T(1,128)} %bitcast.7, s32[1,8,16]{2,1,0:T(8,128)} %left_hbm.1, s32[1,8,16]{2,1,0:T(8,128)} %right_hbm.1, s32[8,128]{1,0:T(8,128)} %pad_add_fusion.meta_hbm, bf16[4,128,2048]{2,1,0:T(8,128)(2,1)} %basis_hbm.1), custom_call_target="tpu_custom_call" | custom-call | flops 4000000000 | bytes 4000000 | tf_op jit(solution)/shard_map/pallas_call | solution.py:437
  90.6 1.5 %copy.10 = f32[8,2048]{1,0:T(8,128)} copy(f32[8,2048]{1,0:T(8,128)} %shard_map.82) | data formatting | bytes 131072

commit v3 on v2

--- a/solution.py
+++ b/solution.py
@@ -121,9 +121,6 @@
     ]
     for q in loads:
         q.start()
-    for q in loads[:5]:
-        q.wait()
-    w[...] = (coeffs[...].astype(jnp.float32) * occ[...]).astype(jnp.bfloat16)
     pl.semaphore_wait(barrier, len(peers))
 
     pending = []
@@ -140,9 +137,13 @@
     m_x = [
         remote(mx.at[x], mx.at[x], m_send.at[d], m_recv.at[d], dev_x((x + d) % NX)) for d in X_ORDER
     ]
-    g_s.start()
-    for q in g_p + m_x:
-        q.start()
+    for q in g_p + [g_s]:
+        q.start()
+    for q in loads[:5]:
+        q.wait()
+    for q in m_x:
+        q.start()
+    w[...] = (coeffs[...].astype(jnp.float32) * occ[...]).astype(jnp.bfloat16)
 
     def compute_tiles(panel, h, s):
         def one(p, carry):
@@ -154,7 +155,7 @@
             tiles[h, p // 4, p % 4] = t.astype(jnp.bfloat16)
             return carry
 
-        lax.fori_loop(0, NTP, one, 0)
+        lax.fori_loop(0, NTP, one, 0, unroll=4)
 
     x1 = {}
     x2c = {}
@@ -183,7 +184,7 @@
         x2c[h] = (to_r, to_l)
 
     def z_copy(h, i):
-        to = 4 * (h % 2) + i
+        to = 2 * i + h % 2
         return remote(
             zs.at[h, i], rz.at[h // 2, z], z_send.at[h, i], z_recv.at[h // 2, z], dev_z(to)
         )
@@ -198,7 +199,7 @@
                 + x2_r[h, i].astype(jnp.float32)
             ).astype(jnp.bfloat16)
             zs[h, i] = total
-            to = 4 * (h % 2) + i
+            to = 2 * i + h % 2
 
             @pl.when(z != to)
             def _():
@@ -211,12 +212,12 @@
     def z_drain(h):
         for i in range(4):
 
-            @pl.when(z != 4 * (h % 2) + i)
+            @pl.when(z != 2 * i + h % 2)
             def _():
                 z_copy(h, i).wait_send()
 
-    sj = z // 4
-    si = z % 4
+    sj = z % 2
+    si = z // 2
 
     def panel_of(k, j):
         if k == 0:
@@ -275,8 +276,11 @@
             e_copy(k, d).start()
         arr[k, band] = send_e[k, band]
 
+    z_at = [lax.rem(z + d, NZ) for d in range(NZ)]
+    x_at = [lax.rem(x + d, NX) for d in range(NX)]
+
     def e_copy(k, d):
-        zz, xx = (z + d // NX) % NZ, (x + d) % NX
+        zz, xx = z_at[d // NX], x_at[d % NX]
         return remote(
             send_e.at[k, zz * NX + xx],
             arr.at[k, band],
@@ -294,8 +298,8 @@
 
         def one(i, acc):
             zf, xf = i // NX, i % NX
-            jj = zf // 4
-            ii = zf % 4
+            jj = zf % 2
+            ii = zf // 2
             s = panel_of(k, 0) * (1 - jj) + panel_of(k, 1) * jj
             val = arr[k, i].astype(jnp.float32)
             slot = hits[s * NX + xf, pl.ds(ii, 1), :]

time: 92.2 us -> 85.3 us (0.925)
  Pallas kernels: 89.2 us -> 82.3 us
    pallas_call x1, Pallas kernels: 89.2 us -> 82.3 us  [body(): pl.pallas_call(kernel, out_shape=jax.ShapeDtypeStruct((NBR, G), f32), in_...]
where the time goes in v3:
time: 85.3 us; the launch traced here: 85.1 us
  Pallas kernels  82.3 us (96%)
  local copies, waits for them, and re-layouts  1.47 us (2%)
  other arithmetic  1.38 us (2%)
    pallas_call x1, Pallas kernels, body(): pl.pallas_call(kernel, out_shape=jax.ShapeDtypeStruct((NBR, G), f32), in_...  82.3 us

profile of v3, /device:TPU:32, one launch (start us, length us, event | category | flops | bytes accessed | tf_op | source)
XLA Modules:
  0.0 85.1 jit_solution(8203230222750298595)
XLA Ops:
  0.0 1.4 %pad_add_fusion.meta_hbm = s32[8,128]{1,0:T(8,128)} fusion(s32[8,6]{1,0:T(8,128)} %bitcast.5, s32[4,6]{1,0:T(4,128)} %param.13, s32[4,6]{1,0:T(4,128)} %param.12), kind=kLoop, calls=%fused_computation | loop fusion | flops 2048 | bytes 4480 | tf_op jit(solution)/shard_map/add | solution.py:433
  1.4 82.3 %shard_map.82 = f32[8,2048]{1,0:T(8,128)} custom-call(bf16[8,128,512]{2,1,0:T(8,128)(2,1)} %bitcast.6, f32[1,512]{1,0:T(1,128)} %bitcast.7, s32[1,8,16]{2,1,0:T(8,128)} %left_hbm.1, s32[1,8,16]{2,1,0:T(8,128)} %right_hbm.1, s32[8,128]{1,0:T(8,128)} %pad_add_fusion.meta_hbm, bf16[4,128,2048]{2,1,0:T(8,128)(2,1)} %basis_hbm.1), custom_call_target="tpu_custom_call" | custom-call | flops 4000000000 | bytes 4000000 | tf_op jit(solution)/shard_map/pallas_call | solution.py:441
  83.7 1.5 %copy.10 = f32[8,2048]{1,0:T(8,128)} copy(f32[8,2048]{1,0:T(8,128)} %shard_map.82) | data formatting | bytes 131072

commit v4 on v3

--- a/solution.py
+++ b/solution.py
@@ -102,7 +102,8 @@
 
     barrier = pltpu.get_barrier_semaphore()
     peers = [sib, dyp, dym]
-    peers += [dev_at((z + d // NX) % NZ, (x + d) % NX) for d in range(1, NX * NZ)]
+    peers += [dev_x((x + d) % NX) for d in X_ORDER]
+    peers += [dev_z((z + d) % NZ) for d in Z_ORDER]
     for p in peers:
         pl.semaphore_signal(barrier, inc=1, device_id=p, device_id_type=MESH)
 
@@ -260,7 +261,7 @@
                     terms[k, t, pl.ds(ch * (CHUNK // GL) + q, 1), :] = row[:, q * GL : (q + 1) * GL]
             return carry
 
-        lax.fori_loop(0, TOP, one, 0)
+        lax.fori_loop(0, TOP, one, 0, unroll=True)
         vals = [terms[k, t] for t in range(TOP)]
         own = [meta_s[k, si, t] for t in range(TOP)]
 
@@ -271,7 +272,7 @@
             send_e[k, o] = acc.astype(jnp.bfloat16)
             return carry
 
-        lax.fori_loop(0, NX * NZ, place, 0)
+        lax.fori_loop(0, NX * NZ, place, 0, unroll=4)
         for d in E_ORDER:
             e_copy(k, d).start()
         arr[k, band] = send_e[k, band]
@@ -305,7 +306,7 @@
             slot = hits[s * NX + xf, pl.ds(ii, 1), :]
             return tuple(acc[b] + jnp.where(slot == float(b), val, 0.0) for b in range(NBR))
 
-        return lax.fori_loop(0, NX * NZ, one, acc)
+        return lax.fori_loop(0, NX * NZ, one, acc, unroll=4)
 
     def to_sibling(src, dst, i, at):
         q = remote(src.at[halves[i]], dst.at[halves[i]], g_send.at[at], g_recv.at[at], sib)

time: 85.3 us -> 82.6 us (0.968)
  Pallas kernels: 82.3 us -> 79.6 us
    pallas_call x1, Pallas kernels: 82.3 us -> 79.6 us  [body(): pl.pallas_call(kernel, out_shape=jax.ShapeDtypeStruct((NBR, G), f32), in_...]
where the time goes in v4:
time: 82.6 us; the launch traced here: 82.4 us
  Pallas kernels  79.6 us (96%)
  local copies, waits for them, and re-layouts  1.47 us (2%)
  other arithmetic  1.38 us (2%)
    pallas_call x1, Pallas kernels, body(): pl.pallas_call(kernel, out_shape=jax.ShapeDtypeStruct((NBR, G), f32), in_...  79.6 us

profile of v4, /device:TPU:32, one launch (start us, length us, event | category | flops | bytes accessed | tf_op | source)
XLA Modules:
  0.0 82.4 jit_solution(10025154868669918145)
XLA Ops:
  0.0 1.4 %pad_add_fusion.meta_hbm = s32[8,128]{1,0:T(8,128)} fusion(s32[8,6]{1,0:T(8,128)} %bitcast.5, s32[4,6]{1,0:T(4,128)} %param.13, s32[4,6]{1,0:T(4,128)} %param.12), kind=kLoop, calls=%fused_computation | loop fusion | flops 2048 | bytes 4480 | tf_op jit(solution)/shard_map/add | solution.py:434
  1.4 79.6 %shard_map.82 = f32[8,2048]{1,0:T(8,128)} custom-call(bf16[8,128,512]{2,1,0:T(8,128)(2,1)} %bitcast.6, f32[1,512]{1,0:T(1,128)} %bitcast.7, s32[1,8,16]{2,1,0:T(8,128)} %left_hbm.1, s32[1,8,16]{2,1,0:T(8,128)} %right_hbm.1, s32[8,128]{1,0:T(8,128)} %pad_add_fusion.meta_hbm, bf16[4,128,2048]{2,1,0:T(8,128)(2,1)} %basis_hbm.1), custom_call_target="tpu_custom_call" | custom-call | flops 4000000000 | bytes 4000000 | tf_op jit(solution)/shard_map/pallas_call | solution.py:442
  81.0 1.5 %copy.10 = f32[8,2048]{1,0:T(8,128)} copy(f32[8,2048]{1,0:T(8,128)} %shard_map.82) | data formatting | bytes 131072

commit v5 on v4

--- a/solution.py
+++ b/solution.py
@@ -27,7 +27,9 @@
     occ_hbm,
     left_hbm,
     right_hbm,
-    meta_hbm,
+    owners_hbm,
+    slots_hbm,
+    patterns_hbm,
     basis_hbm,
     out,
     coeffs,
@@ -51,8 +53,11 @@
     terms,
     send_e,
     arr,
-    mx,
+    owners_v,
+    slots_v,
+    patterns_v,
     mz,
+    mall,
     hits,
     meta_s,
     left_s,
@@ -79,6 +84,8 @@
     oc = 1 - c
     xr, xl, x2 = (x + 1) % NX, (x + 3) % NX, (x + 2) % NX
 
+    zr, zl = (z + 1) % NZ, (z + NZ - 1) % NZ
+
     def dev_row(rr):
         return (rr, band)
 
@@ -102,8 +109,7 @@
 
     barrier = pltpu.get_barrier_semaphore()
     peers = [sib, dyp, dym]
-    peers += [dev_x((x + d) % NX) for d in X_ORDER]
-    peers += [dev_z((z + d) % NZ) for d in Z_ORDER]
+    peers += [dev_x(xr), dev_x(xl), dev_z(zr), dev_z(zl)]
     for p in peers:
         pl.semaphore_signal(barrier, inc=1, device_id=p, device_id_type=MESH)
 
@@ -115,7 +121,9 @@
                 (occ_hbm, occ),
                 (left_hbm, left_s),
                 (right_hbm, right_s),
-                (meta_hbm, mx.at[x]),
+                (owners_hbm, owners_v),
+                (slots_hbm, slots_v),
+                (patterns_hbm, patterns_v),
                 (basis_hbm, basis),
             )
         )
@@ -135,15 +143,27 @@
         remote(coeffs_hbm.at[v], s_a.at[v], g_send.at[3 + i], g_recv.at[3 + i], dym)
         for i, v in enumerate(halves)
     ]
-    m_x = [
-        remote(mx.at[x], mx.at[x], m_send.at[d], m_recv.at[d], dev_x((x + d) % NX)) for d in X_ORDER
-    ]
     for q in g_p + [g_s]:
         q.start()
-    for q in loads[:5]:
+    for q in loads[:7]:
         q.wait()
-    for q in m_x:
-        q.start()
+    mz[z] = jnp.zeros((2, 8, 128), jnp.int32)
+    mz[z, 0, pl.ds(0, 4), pl.ds(0, TOP)] = owners_v[...]
+    mz[z, 0, pl.ds(4, 4), pl.ds(0, TOP)] = slots_v[...]
+    mz[z, 1, :, pl.ds(0, TOP)] = patterns_v[...]
+
+    def meta_z(step):
+        at = (z + NZ - step) % NZ
+        to = [remote(mz.at[at], mz.at[at], m_send.at[step], m_recv.at[step], dev_z(zr))]
+        if step < 3:
+            at = (z + step) % NZ
+            i = 4 + step
+            to.append(remote(mz.at[at], mz.at[at], m_send.at[i], m_recv.at[i], dev_z(zl)))
+        for q in to:
+            q.start()
+        return to
+
+    m_z = [meta_z(0)]
     w[...] = (coeffs[...].astype(jnp.float32) * occ[...]).astype(jnp.bfloat16)
 
     def compute_tiles(panel, h, s):
@@ -250,8 +270,8 @@
         scale = jnp.where(same, 1.0, 2.0).astype(jnp.float32)
 
         def one(t, carry):
-            pa = meta_s[k, 2 * si, 12 + t]
-            pb = meta_s[k, 2 * si + 1, 12 + t]
+            pa = meta_s[k, 1, 2 * si, t]
+            pb = meta_s[k, 1, 2 * si + 1, t]
             for ch in range(G // CHUNK):
                 cols = pl.ds(ch * CHUNK, CHUNK)
                 prod = jnp.dot(block, basis[pb, :, cols], preferred_element_type=jnp.float32)
@@ -263,7 +283,7 @@
 
         lax.fori_loop(0, TOP, one, 0, unroll=True)
         vals = [terms[k, t] for t in range(TOP)]
-        own = [meta_s[k, si, t] for t in range(TOP)]
+        own = [meta_s[k, 0, si, t] for t in range(TOP)]
 
         def place(o, carry):
             acc = jnp.zeros((GS, GL), jnp.float32)
@@ -303,56 +323,57 @@
             ii = zf // 2
             s = panel_of(k, 0) * (1 - jj) + panel_of(k, 1) * jj
             val = arr[k, i].astype(jnp.float32)
-            slot = hits[s * NX + xf, pl.ds(ii, 1), :]
+            slot = hits[xf * NZ + s, pl.ds(ii, 1), :]
             return tuple(acc[b] + jnp.where(slot == float(b), val, 0.0) for b in range(NBR))
 
         return lax.fori_loop(0, NX * NZ, one, acc, unroll=4)
 
-    def to_sibling(src, dst, i, at):
-        q = remote(src.at[halves[i]], dst.at[halves[i]], g_send.at[at], g_recv.at[at], sib)
+    pieces = halves[:1] + (pl.ds(4, 2), pl.ds(6, 2))
+
+    def to_sibling(src, dst, v, at):
+        q = remote(src.at[v], dst.at[v], g_send.at[at], g_recv.at[at], sib)
         q.start()
         return q
 
     compute_tiles(coeffs, 0, panel_of(0, 0))
     x1_start(0)
-    for m in m_x:
-        m.wait_recv()
-    m_z = []
-    for d in Z_ORDER:
-        to = (z + d) % NZ
-        q = remote(mx, mz.at[z], m_send.at[4 + d], m_recv.at[4 + d], dev_z(to))
-        q.start()
-        m_z.append(q)
-    mz[z] = mx[...]
     g_s.wait_recv()
     compute_tiles(b0, 1, panel_of(0, 1))
     x1_start(1)
+
+    def next_meta(step):
+        for q in m_z[step - 1]:
+            q.wait_recv()
+        if step < 4:
+            m_z.append(meta_z(step))
+
+    next_meta(1)
     x2_start(0)
     g_p[0].wait_recv()
     for q in g_m:
         q.start()
-    g_fs = [to_sibling(f_a, f_b, 0, 5)]
+    g_fs = [to_sibling(f_a, f_b, halves[0], 5)]
+    next_meta(2)
     x2_start(1)
-    for q in m_z:
-        q.wait_recv()
+    next_meta(3)
+
+    g_p[1].wait_recv()
+    g_fs.append(to_sibling(f_a, f_b, halves[1], 6))
+    compute_tiles(f_a, 2, panel_of(1, 0))
+    x1_start(2)
+    next_meta(4)
     locals_ = []
     for k in range(4):
-        q = pltpu.make_async_copy(mz.at[my_panel(k), x], meta_s.at[k], l_sem.at[k])
+        q = pltpu.make_async_copy(mz.at[my_panel(k)], meta_s.at[k], l_sem.at[k])
         q.start()
         locals_.append(q)
-    lane = lax.broadcasted_iota(jnp.int32, (NX * NZ, 8, 128), 2)
-    every = mz[...].reshape(NX * NZ, 8, 128)
-    slots = pltpu.roll(every, 128 - TOP, axis=2)
-    mine = jnp.logical_and(lane < TOP, every == band)
-    found = jnp.where(mine, slots + 1, 0).astype(jnp.bfloat16).reshape(NX * NZ * 8, 128)
-    ones = jnp.ones((128, 128), jnp.bfloat16)
-    found = jnp.dot(found, ones, preferred_element_type=jnp.float32) - 1.0
-    hits[...] = found.reshape(NX * NZ, 8, 128)
-
-    g_p[1].wait_recv()
-    g_fs.append(to_sibling(f_a, f_b, 1, 6))
-    compute_tiles(f_a, 2, panel_of(1, 0))
-    x1_start(2)
+    mall[x] = mz[:, 0]
+    m_x = [
+        remote(mall.at[x], mall.at[x], m_send.at[7 + i], m_recv.at[7 + i], dev_x(to))
+        for i, to in enumerate((xr, xl))
+    ]
+    for q in m_x:
+        q.start()
     z_start(0)
     for q in g_fs:
         q.wait_recv()
@@ -361,20 +382,24 @@
     g_m[0].wait_recv()
     g_f = [
         remote(f_a.at[v], t_a.at[v], g_send.at[7 + i], g_recv.at[7 + i], dyp)
-        for i, v in enumerate(halves)
+        for i, v in enumerate(pieces)
     ]
     for q in g_f:
         q.start()
-    g_ms = [to_sibling(s_a, s_b, 0, 9)]
+    g_ms = [to_sibling(s_a, s_b, halves[0], 10)]
     z_start(1)
     x2_start(2)
     x2_start(3)
+    for q in m_x:
+        q.wait_recv()
+    m_x.append(remote(mall.at[xl], mall.at[xl], m_send.at[9], m_recv.at[9], dev_x(xr)))
+    m_x[2].start()
     for q in locals_:
         q.wait()
-    loads[5].wait()
+    loads[7].wait()
 
     g_m[1].wait_recv()
-    g_ms.append(to_sibling(s_a, s_b, 1, 10))
+    g_ms.append(to_sibling(s_a, s_b, halves[1], 11))
     compute_tiles(s_a, 4, panel_of(2, 0))
     x1_start(4)
     z_start(2)
@@ -383,14 +408,24 @@
     compute_tiles(s_b, 5, panel_of(2, 1))
     x1_start(5)
     g_f[0].wait_recv()
-    g_ts = [to_sibling(t_a, t_b, 0, 11)]
+    g_ts = [to_sibling(t_a, t_b, pieces[0], 12)]
     z_start(3)
     x2_start(4)
     collocate(0)
     x2_start(5)
-
-    g_f[1].wait_recv()
-    g_ts.append(to_sibling(t_a, t_b, 1, 12))
+    m_x[2].wait_recv()
+    lane = lax.broadcasted_iota(jnp.int32, (NX * NZ, 8, 128), 2)
+    every = mall[...].reshape(NX * NZ, 8, 128)
+    slots = pltpu.roll(every, 4, axis=1)
+    mine = jnp.logical_and(lane < TOP, every == band)
+    found = jnp.where(mine, slots + 1, 0).astype(jnp.bfloat16).reshape(NX * NZ * 8, 128)
+    ones = jnp.ones((128, 128), jnp.bfloat16)
+    found = jnp.dot(found, ones, preferred_element_type=jnp.float32) - 1.0
+    hits[...] = found.reshape(NX * NZ, 8, 128)
+
+    for i in (1, 2):
+        g_f[i].wait_recv()
+        g_ts.append(to_sibling(t_a, t_b, pieces[i], 12 + i))
     compute_tiles(t_a, 6, panel_of(3, 0))
     x1_start(6)
     z_start(4)
@@ -415,7 +450,7 @@
         for q in range(GS):
             out[pl.ds(b, 1), pl.ds(q * GL, GL)] = acc[b][q : q + 1, :]
 
-    pending += [g_s] + g_p + g_m + g_fs + g_f + g_ms + g_ts + m_x + m_z
+    pending += [g_s] + g_p + g_m + g_fs + g_f + g_ms + g_ts + m_x + sum(m_z, [])
     for h in range(8):
         pending += list(x1[h]) + list(x2c[h])
     for q in pending:
@@ -427,14 +462,6 @@
 
 
 def body(coeffs, occupation, tile_left, tile_right, owners, brick_slot, patterns, basis_table):
-    def place(a, at):
-        return jnp.pad(a, ((0, 8 - a.shape[0]), (at, 128 - TOP - at)))
-
-    meta = (
-        place(owners, 0)
-        + place(brick_slot, TOP)
-        + place(jnp.transpose(patterns, (0, 2, 1)).reshape(8, TOP), 2 * TOP)
-    )
     hbm = pl.BlockSpec(memory_space=pltpu.HBM)
     bf, f32 = jnp.bfloat16, jnp.float32
     panel = pltpu.VMEM((BLOCKS, BS, KD), bf)
@@ -442,7 +469,7 @@
     out = pl.pallas_call(
         kernel,
         out_shape=jax.ShapeDtypeStruct((NBR, G), f32),
-        in_specs=[hbm] * 6,
+        in_specs=[hbm] * 8,
         out_specs=pl.BlockSpec(memory_space=pltpu.VMEM),
         scratch_shapes=[
             panel,
@@ -461,24 +488,27 @@
             pltpu.VMEM((4, TOP, GS, GL), f32),
             pltpu.VMEM((4, NX * NZ, GS, GL), bf),
             pltpu.VMEM((4, NX * NZ, GS, GL), bf),
-            pltpu.VMEM((NX, 8, 128), jnp.int32),
-            pltpu.VMEM((NZ, NX, 8, 128), jnp.int32),
+            pltpu.VMEM((4, TOP), jnp.int32),
+            pltpu.VMEM((4, TOP), jnp.int32),
+            pltpu.VMEM((8, TOP), jnp.int32),
+            pltpu.VMEM((NZ, 2, 8, 128), jnp.int32),
+            pltpu.VMEM((NX, NZ, 8, 128), jnp.int32),
             pltpu.VMEM((NX * NZ, 8, 128), f32),
-            pltpu.SMEM((4, 8, 128), jnp.int32),
+            pltpu.SMEM((4, 2, 8, 128), jnp.int32),
             pltpu.SMEM((1, 8, NTP), jnp.int32),
             pltpu.SMEM((1, 8, NTP), jnp.int32),
-            dma((13,)),
-            dma((13,)),
+            dma((15,)),
+            dma((15,)),
             dma((8, 4)),
             dma((8, 4)),
             dma((8, 4)),
             dma((4, NZ)),
             dma((4,)),
             dma((4,)),
-            dma((12,)),
-            dma((12,)),
+            dma((10,)),
+            dma((10,)),
             dma((4,)),
-            dma((6,)),
+            dma((8,)),
         ],
         compiler_params=pltpu.CompilerParams(
             collective_id=0, has_side_effects=True, vmem_limit_bytes=VMEM
@@ -491,7 +521,9 @@
         occupation.reshape(1, KD),
         tile_left,
         tile_right,
-        meta,
+        owners,
+        brick_slot,
+        jnp.transpose(patterns, (0, 2, 1)).reshape(8, TOP),
         basis_table,
     )
     return out

time: 82.6 us -> 80.2 us (0.971)
  Pallas kernels: 79.6 us -> 77.8 us
  other arithmetic: 1.38 us -> 0 us
    pallas_call x1, Pallas kernels: 79.6 us -> 77.8 us  [body(): pl.pallas_call(kernel, out_shape=jax.ShapeDtypeStruct((NBR, G), f32), in_...]
    add x1 -> x0, other arithmetic: 1.38 us -> none  [body(): place(owners, 0) + place(brick_slot, TOP)]
where the time goes in v5:
time: 80.2 us; the launch traced here: 79.3 us
  Pallas kernels  77.8 us (97%)
  local copies, waits for them, and re-layouts  1.47 us (2%)
    pallas_call x1, Pallas kernels, body(): pl.pallas_call(kernel, out_shape=jax.ShapeDtypeStruct((NBR, G), f32), in_...  77.8 us

profile of v5, /device:TPU:32, one launch (start us, length us, event | category | flops | bytes accessed | tf_op | source)
XLA Modules:
  0.0 79.3 jit_solution(15475932484045921525)
XLA Ops:
  0.0 77.8 %shard_map.82 = f32[8,2048]{1,0:T(8,128)} custom-call(bf16[8,128,512]{2,1,0:T(8,128)(2,1)} %bitcast.5, f32[1,512]{1,0:T(1,128)} %bitcast.7, s32[1,8,16]{2,1,0:T(8,128)} %left_hbm.1, s32[1,8,16]{2,1,0:T(8,128)} %right_hbm.1, s32[4,6]{1,0:T(4,128)} %owners_hbm.1, s32[4,6]{1,0:T(4,128)} %slots_hbm.1, s32[8,6]{1,0:T(8,128)} %bitcast.6, ...), custom_call_target="tpu_custom_call" | custom-call | flops 4000000000 | bytes 4000000 | tf_op jit(solution)/shard_map/pallas_call | solution.py:469
  77.8 1.5 %copy.10 = f32[8,2048]{1,0:T(8,128)} copy(f32[8,2048]{1,0:T(8,128)} %shard_map.82) | data formatting | bytes 131072

commit v6 on v5

--- a/solution.py
+++ b/solution.py
@@ -176,9 +176,10 @@
             tiles[h, p // 4, p % 4] = t.astype(jnp.bfloat16)
             return carry
 
-        lax.fori_loop(0, NTP, one, 0, unroll=4)
+        lax.fori_loop(0, NTP, one, 0, unroll=8)
 
     x1 = {}
+    xo = {}
     x2c = {}
     top, low = pl.ds(0, 2), pl.ds(2, 2)
 
@@ -187,12 +188,24 @@
             remote(tiles.at[h, x2, top], x1_l.at[h], x_send.at[h, 0], x_recv.at[h, 0], dev_x(xr)),
             remote(tiles.at[h, x2, low], x1_r.at[h], x_send.at[h, 1], x_recv.at[h, 1], dev_x(xl)),
         )
-        for q in x1[h]:
+        xo[h] = (
+            remote(
+                tiles.at[h, xr, low], x2_l.at[h, low], x_send.at[h, 4], x_recv.at[h, 4], dev_x(xr)
+            ),
+            remote(
+                tiles.at[h, xl, top], x2_r.at[h, top], x_send.at[h, 5], x_recv.at[h, 5], dev_x(xl)
+            ),
+        )
+        for q in x1[h] + xo[h]:
             q.start()
 
     def x2_start(h):
-        to_r = remote(tiles.at[h, xr], x2_l.at[h], x_send.at[h, 2], x_recv.at[h, 2], dev_x(xr))
-        to_l = remote(tiles.at[h, xl], x2_r.at[h], x_send.at[h, 3], x_recv.at[h, 3], dev_x(xl))
+        to_r = remote(
+            tiles.at[h, xr, top], x2_l.at[h, top], x_send.at[h, 2], x_recv.at[h, 2], dev_x(xr)
+        )
+        to_l = remote(
+            tiles.at[h, xl, low], x2_r.at[h, low], x_send.at[h, 3], x_recv.at[h, 3], dev_x(xl)
+        )
         for part, dst, got, first, second in (
             (top, xr, x1_l, x1[h][0], to_r),
             (low, xl, x1_r, x1[h][1], to_l),
@@ -211,7 +224,7 @@
         )
 
     def z_start(h):
-        for q in x2c[h]:
+        for q in xo[h] + x2c[h]:
             q.wait_recv()
         for i in range(4):
             total = (
@@ -428,11 +441,11 @@
         g_ts.append(to_sibling(t_a, t_b, pieces[i], 12 + i))
     compute_tiles(t_a, 6, panel_of(3, 0))
     x1_start(6)
-    z_start(4)
     for q in g_ts:
         q.wait_recv()
     compute_tiles(t_b, 7, panel_of(3, 1))
     x1_start(7)
+    z_start(4)
     z_start(5)
     x2_start(6)
     x2_start(7)
@@ -452,7 +465,7 @@
 
     pending += [g_s] + g_p + g_m + g_fs + g_f + g_ms + g_ts + m_x + sum(m_z, [])
     for h in range(8):
-        pending += list(x1[h]) + list(x2c[h])
+        pending += list(x1[h] + xo[h] + x2c[h])
     for q in pending:
         q.wait_send()
     for h in range(8):
@@ -499,8 +512,8 @@
             pltpu.SMEM((1, 8, NTP), jnp.int32),
             dma((15,)),
             dma((15,)),
-            dma((8, 4)),
-            dma((8, 4)),
+            dma((8, 6)),
+            dma((8, 6)),
             dma((8, 4)),
             dma((4, NZ)),
             dma((4,)),

time: 80.2 us -> 79.6 us (level)
  no operation moved by 1% of the time
where the time goes in v6:
time: 79.6 us; the launch traced here: 78.8 us
  Pallas kernels  77.3 us (97%)
  local copies, waits for them, and re-layouts  1.47 us (2%)
    pallas_call x1, Pallas kernels, body(): pl.pallas_call(kernel, out_shape=jax.ShapeDtypeStruct((NBR, G), f32), in_...  77.3 us

profile of v6, /device:TPU:32, one launch (start us, length us, event | category | flops | bytes accessed | tf_op | source)
XLA Modules:
  0.0 78.8 jit_solution(4969990485248172503)
XLA Ops:
  0.0 77.3 %shard_map.82 = f32[8,2048]{1,0:T(8,128)} custom-call(bf16[8,128,512]{2,1,0:T(8,128)(2,1)} %bitcast.5, f32[1,512]{1,0:T(1,128)} %bitcast.7, s32[1,8,16]{2,1,0:T(8,128)} %left_hbm.1, s32[1,8,16]{2,1,0:T(8,128)} %right_hbm.1, s32[4,6]{1,0:T(4,128)} %owners_hbm.1, s32[4,6]{1,0:T(4,128)} %slots_hbm.1, s32[8,6]{1,0:T(8,128)} %bitcast.6, ...), custom_call_target="tpu_custom_call" | custom-call | flops 4000000000 | bytes 4000000 | tf_op jit(solution)/shard_map/pallas_call | solution.py:482
  77.3 1.5 %copy.10 = f32[8,2048]{1,0:T(8,128)} copy(f32[8,2048]{1,0:T(8,128)} %shard_map.82) | data formatting | bytes 131072

commit v7 on v6

--- a/solution.py
+++ b/solution.py
@@ -133,15 +133,16 @@
     pl.semaphore_wait(barrier, len(peers))
 
     pending = []
+    pieces = (pl.ds(0, 4), pl.ds(4, 2), pl.ds(6, 2))
     halves = (pl.ds(0, BLOCKS // 2), pl.ds(BLOCKS // 2, BLOCKS // 2))
     g_s = remote(coeffs_hbm, b0, g_send.at[0], g_recv.at[0], sib)
     g_p = [
-        remote(coeffs_hbm.at[v], f_a.at[v], g_send.at[1 + i], g_recv.at[1 + i], dyp)
-        for i, v in enumerate(halves)
+        remote(coeffs_hbm.at[v], f_a.at[v], g_send.at[15 + i], g_recv.at[15 + i], dyp)
+        for i, v in enumerate(pieces)
     ]
     g_m = [
-        remote(coeffs_hbm.at[v], s_a.at[v], g_send.at[3 + i], g_recv.at[3 + i], dym)
-        for i, v in enumerate(halves)
+        remote(coeffs_hbm.at[v], s_a.at[v], g_send.at[18 + i], g_recv.at[18 + i], dym)
+        for i, v in enumerate(pieces)
     ]
     for q in g_p + [g_s]:
         q.start()
@@ -298,16 +299,16 @@
         vals = [terms[k, t] for t in range(TOP)]
         own = [meta_s[k, 0, si, t] for t in range(TOP)]
 
-        def place(o, carry):
+        def place(o):
             acc = jnp.zeros((GS, GL), jnp.float32)
             for t in range(TOP):
                 acc = jnp.where(own[t] == o, vals[t], acc)
             send_e[k, o] = acc.astype(jnp.bfloat16)
-            return carry
-
-        lax.fori_loop(0, NX * NZ, place, 0, unroll=4)
+
         for d in E_ORDER:
+            place(z_at[d // NX] * NX + x_at[d % NX])
             e_copy(k, d).start()
+        place(band)
         arr[k, band] = send_e[k, band]
 
     z_at = [lax.rem(z + d, NZ) for d in range(NZ)]
@@ -341,7 +342,6 @@
 
         return lax.fori_loop(0, NX * NZ, one, acc, unroll=4)
 
-    pieces = halves[:1] + (pl.ds(4, 2), pl.ds(6, 2))
 
     def to_sibling(src, dst, v, at):
         q = remote(src.at[v], dst.at[v], g_send.at[at], g_recv.at[at], sib)
@@ -363,14 +363,15 @@
     next_meta(1)
     x2_start(0)
     g_p[0].wait_recv()
+    g_fs = [to_sibling(f_a, f_b, halves[0], 5)]
+    g_p[1].wait_recv()
     for q in g_m:
         q.start()
-    g_fs = [to_sibling(f_a, f_b, halves[0], 5)]
     next_meta(2)
     x2_start(1)
     next_meta(3)
 
-    g_p[1].wait_recv()
+    g_p[2].wait_recv()
     g_fs.append(to_sibling(f_a, f_b, halves[1], 6))
     compute_tiles(f_a, 2, panel_of(1, 0))
     x1_start(2)
@@ -393,6 +394,7 @@
     compute_tiles(f_b, 3, panel_of(1, 1))
     x1_start(3)
     g_m[0].wait_recv()
+    g_m[1].wait_recv()
     g_f = [
         remote(f_a.at[v], t_a.at[v], g_send.at[7 + i], g_recv.at[7 + i], dyp)
         for i, v in enumerate(pieces)
@@ -411,7 +413,7 @@
         q.wait()
     loads[7].wait()
 
-    g_m[1].wait_recv()
+    g_m[2].wait_recv()
     g_ms.append(to_sibling(s_a, s_b, halves[1], 11))
     compute_tiles(s_a, 4, panel_of(2, 0))
     x1_start(4)
@@ -510,8 +512,8 @@
             pltpu.SMEM((4, 2, 8, 128), jnp.int32),
             pltpu.SMEM((1, 8, NTP), jnp.int32),
             pltpu.SMEM((1, 8, NTP), jnp.int32),
-            dma((15,)),
-            dma((15,)),
+            dma((21,)),
+            dma((21,)),
             dma((8, 6)),
             dma((8, 6)),
             dma((8, 4)),

time: 79.6 us -> 78.2 us (0.982)
  Pallas kernels: 77.3 us -> 76.2 us
    pallas_call x1, Pallas kernels: 77.3 us -> 76.2 us  [body(): pl.pallas_call(kernel, out_shape=jax.ShapeDtypeStruct((NBR, G), f32), in_...]
where the time goes in v7:
time: 78.2 us; the launch traced here: 77.7 us
  Pallas kernels  76.2 us (97%)
  local copies, waits for them, and re-layouts  1.47 us (2%)
    pallas_call x1, Pallas kernels, body(): pl.pallas_call(kernel, out_shape=jax.ShapeDtypeStruct((NBR, G), f32), in_...  76.2 us

profile of v7, /device:TPU:32, one launch (start us, length us, event | category | flops | bytes accessed | tf_op | source)
XLA Modules:
  0.0 77.7 jit_solution(2167093031153002436)
XLA Ops:
  0.0 76.2 %shard_map.82 = f32[8,2048]{1,0:T(8,128)} custom-call(bf16[8,128,512]{2,1,0:T(8,128)(2,1)} %bitcast.5, f32[1,512]{1,0:T(1,128)} %bitcast.7, s32[1,8,16]{2,1,0:T(8,128)} %left_hbm.1, s32[1,8,16]{2,1,0:T(8,128)} %right_hbm.1, s32[4,6]{1,0:T(4,128)} %owners_hbm.1, s32[4,6]{1,0:T(4,128)} %slots_hbm.1, s32[8,6]{1,0:T(8,128)} %bitcast.6, ...), custom_call_target="tpu_custom_call" | custom-call | flops 4000000000 | bytes 4000000 | tf_op jit(solution)/shard_map/pallas_call | solution.py:484
  76.3 1.5 %copy.10 = f32[8,2048]{1,0:T(8,128)} copy(f32[8,2048]{1,0:T(8,128)} %shard_map.82) | data formatting | bytes 131072

commit v8 on v7

--- a/solution.py
+++ b/solution.py
@@ -458,6 +458,15 @@
     acc = tuple(jnp.zeros((GS, GL), jnp.float32) for _ in range(NBR))
     acc = finish(0, acc)
     acc = finish(1, acc)
+    pending += [g_s] + g_p + g_m + g_fs + g_f + g_ms + g_ts + m_x + sum(m_z, [])
+    for h in range(8):
+        pending += list(x1[h] + xo[h] + x2c[h])
+    for q in pending:
+        q.wait_send()
+    for h in range(7):
+        z_drain(h)
+    for k in (0, 1):
+        e_all(k).wait_send()
     collocate(3)
     acc = finish(2, acc)
     acc = finish(3, acc)
@@ -465,14 +474,8 @@
         for q in range(GS):
             out[pl.ds(b, 1), pl.ds(q * GL, GL)] = acc[b][q : q + 1, :]
 
-    pending += [g_s] + g_p + g_m + g_fs + g_f + g_ms + g_ts + m_x + sum(m_z, [])
-    for h in range(8):
-        pending += list(x1[h] + xo[h] + x2c[h])
-    for q in pending:
-        q.wait_send()
-    for h in range(8):
-        z_drain(h)
-    for k in range(4):
+    z_drain(7)
+    for k in (2, 3):
         e_all(k).wait_send()
 
 

time: 78.2 us -> 78 us (level)
  no operation moved by 1% of the time
where the time goes in v8:
time: 78 us; the launch traced here: 77.6 us
  Pallas kernels  76.1 us (98%)
  local copies, waits for them, and re-layouts  1.47 us (2%)
    pallas_call x1, Pallas kernels, body(): pl.pallas_call(kernel, out_shape=jax.ShapeDtypeStruct((NBR, G), f32), in_...  76.1 us

profile of v8, /device:TPU:32, one launch (start us, length us, event | category | flops | bytes accessed | tf_op | source)
XLA Modules:
  0.0 77.6 jit_solution(17154161171673953414)
XLA Ops:
  0.0 76.1 %shard_map.82 = f32[8,2048]{1,0:T(8,128)} custom-call(bf16[8,128,512]{2,1,0:T(8,128)(2,1)} %bitcast.5, f32[1,512]{1,0:T(1,128)} %bitcast.7, s32[1,8,16]{2,1,0:T(8,128)} %left_hbm.1, s32[1,8,16]{2,1,0:T(8,128)} %right_hbm.1, s32[4,6]{1,0:T(4,128)} %owners_hbm.1, s32[4,6]{1,0:T(4,128)} %slots_hbm.1, s32[8,6]{1,0:T(8,128)} %bitcast.6, ...), custom_call_target="tpu_custom_call" | custom-call | flops 4000000000 | bytes 4000000 | tf_op jit(solution)/shard_map/pallas_call | solution.py:487
  76.1 1.5 %copy.10 = f32[8,2048]{1,0:T(8,128)} copy(f32[8,2048]{1,0:T(8,128)} %shard_map.82) | data formatting | bytes 131072
